TPU v7x, 256 devices: a whole 4x4x8 slice. The times are simulated.
256 devices in a mesh: dp: 16 (over z, x_hi), expert: 16 (over y, x_lo, core).
Axes of the slice: x: 4 (x_hi: 2, x_lo: 2; x = x_hi * 2 + x_lo), y: 4, z: 8, core: 2. Of those that a mesh axis runs over, the one named last changes fastest.
Arguments:
- latent: bfloat16 [3, 8192, 1536], P(None, 'dp'), may hold values from -6 to 6
- query_grad: bfloat16 [3, 8192, 12288], P(None, 'dp', 'expert'), may hold values from -0.15625 to 0.15625
- momentum: float32 [3, 64, 192, 1536], P(None, 'expert', 'dp'), may hold values from -6 to 6
- weight: float32 [3, 64, 192, 1536], P(None, 'expert', 'dp'), may hold values from -6 to 6
- max_logit: float32 [3, 64], P(None, 'expert'), may hold values from 40 to 400
- owner_list: int32 [3, 64], P(None, 'expert'), may hold values from 0 to 15, as said below
Outputs:
- update: float32 [3, 64, 192, 1536], P(None, 'expert', 'dp')
- new_weight: float32 [3, 64, 192, 1536], P(None, 'expert', 'dp')
- new_momentum: float32 [3, 64, 192, 1536], P(None, 'expert', 'dp')
- owned_updates: bfloat16 [16, 32, 192, 1536], P('expert', 'dp')
Inputs may be any that keep to these rules, and one draw needn't show every extreme that they name: `owner_list`: among the 12 matrices of one index of expert no owner is named more than 2 times, and some owner is named exactly 2 times.
All inputs are finite; a program needn't handle non-finite values.
Results may differ from a plain program's by a relative error of at most 0.03.
Values may be sent and summed in bfloat16 or wider, within the bound.
A program may use at most 128 MiB of HBM per device.

v0:
```python
import functools
import math

import jax
import jax.numpy as jnp
import numpy as np
from jax import lax
from jax.experimental import pallas as pl
from jax.experimental.pallas import tpu as pltpu
from jax.sharding import PartitionSpec as P

NOPE = 128
CAP = 2
ITERS = 5
X_HI = 2

DECAY_RATE = 0.95
EPSILON = 1e-07
COEF_LINEAR = 3.4445
COEF_CUBIC = -4.775
COEF_QUINTIC = 2.0315
LEARN_RATE = 0.02
WEIGHT_DECAY = 0.1
CLIP_LIMIT = 100.0
RMS_FACTOR = 0.2

MESH = pl.DeviceIdType.MESH
F32 = jnp.float32
BF16 = jnp.bfloat16


def reorder_matrix(shape, axes):
    picked = np.arange(math.prod(shape)).reshape(shape).transpose(axes).reshape(-1)
    table = np.zeros((picked.size, picked.size), np.float32)
    table[np.arange(picked.size), picked] = 1.0
    return table


def remote(src, dst, send_sem, recv_sem, dp):
    return pltpu.make_async_remote_copy(
        src_ref=src,
        dst_ref=dst,
        send_sem=send_sem,
        recv_sem=recv_sem,
        device_id={"dp": dp},
        device_id_type=MESH,
    )


def full_dot(left, right):
    return jnp.dot(left, right, precision=lax.Precision.HIGHEST, preferred_element_type=F32)


def polynomial(gram):
    size = gram.shape[0]
    rows = lax.broadcasted_iota(jnp.int32, (size, size), 0)
    columns = lax.broadcasted_iota(jnp.int32, (size, size), 1)
    eye = jnp.where(rows == columns, 1.0, 0.0).astype(F32)
    total = None
    for sweep in range(ITERS):
        mixing = COEF_LINEAR * eye + COEF_CUBIC * gram + COEF_QUINTIC * full_dot(gram, gram)
        total = mixing if total is None else full_dot(mixing, total)
        if sweep < ITERS - 1:
            gram = full_dot(full_dot(mixing, gram), mixing)
    return total


def worker_of(layer, head):
    return 4 * head + (layer if layer < 2 else 2 + head % 2)


def orthogonalize(received, gather_ref, shuffled):
    shuffled[...] = jnp.dot(gather_ref[...], received, preferred_element_type=F32).astype(BF16)
    size = shuffled.shape[0] // 4
    gram = jnp.zeros((size, size), F32)
    for q in range(4):
        piece = shuffled[q * size : (q + 1) * size]
        gram = gram + lax.dot_general(
            piece, piece, (((1,), (1,)), ((), ())), preferred_element_type=F32
        )
    on_diagonal = lax.broadcasted_iota(jnp.int32, gram.shape, 0) == lax.broadcasted_iota(
        jnp.int32, gram.shape, 1
    )
    squares = jnp.sum(
        jnp.sum(jnp.where(on_diagonal, gram, 0.0), axis=1, keepdims=True), axis=0, keepdims=True
    )
    scale = 1.0 / (jnp.sqrt(squares) + EPSILON)
    mixed = polynomial(gram * scale * scale) * scale
    high = mixed.astype(BF16)
    low = (mixed - high.astype(F32)).astype(BF16)
    for q in range(4):
        span = slice(q * size, (q + 1) * size)
        piece = shuffled[span]
        shuffled[span] = (
            jnp.dot(high, piece, preferred_element_type=F32)
            + jnp.dot(low, piece, preferred_element_type=F32)
        ).astype(BF16)


def kernel(
    group,
    latent_hbm, grad_hbm, momentum_hbm, by_row_hbm, gather_hbm, spread_hbm, split_hbm, join_hbm, owner_ref,
    new_momentum_hbm, owned_hbm, update_hbm,
    new_momentum_ref, owned_ref, update_ref,
    latent_ref, grad_ref, momentum_ref, by_row_ref, gather_ref, spread_ref, split_ref, join_ref,
    cot, part_a, part_b, part_x, ring_a, ring_b, ring_x, cross_x, pair_a, pair_b,
    total, turned, pick, blocks, outgoing, incoming, shuffled, worked, back, returned,
    load_sem, send_a, got_a, send_b, got_b, send_x, got_x, send_c, got_c, send_p, got_p,
    send_out, got_out, send_work, got_work, send_back, got_back, store_sem,
):
    layers, rows_q, heads, width = momentum_ref.shape
    rows = heads * rows_q
    mats = layers * heads
    ring = group // X_HI
    quarter = width // 4
    half = width // 2
    narrow = part_b.shape[-1]
    extra = part_x.shape[-1] - half
    full_rows = rows_q * group
    me = lax.axis_index("dp")
    z = me // X_HI
    side = me % X_HI
    up = lax.rem(z + 1, ring) * X_HI + side
    down = lax.rem(z + ring - 1, ring) * X_HI + side
    partner = z * X_HI + 1 - side

    barrier = pltpu.get_barrier_semaphore()
    for peer in (up, down, partner):
        pl.semaphore_signal(barrier, inc=1, device_id={"dp": peer}, device_id_type=MESH)

    loads = {}
    for number, (name, src, dst) in enumerate(
        [
            ("by_row", by_row_hbm, by_row_ref),
            ("grad0", grad_hbm.at[0], grad_ref.at[0]),
            ("latent0", latent_hbm.at[0], latent_ref.at[0]),
            ("grad2", grad_hbm.at[2], grad_ref.at[2]),
            ("latent2", latent_hbm.at[2], latent_ref.at[2]),
            ("grad1", grad_hbm.at[1], grad_ref.at[1]),
            ("latent1", latent_hbm.at[1], latent_ref.at[1]),
            ("momentum", momentum_hbm, momentum_ref),
            ("split", split_hbm, split_ref),
            ("gather", gather_hbm, gather_ref),
            ("spread", spread_hbm, spread_ref),
            ("join", join_hbm, join_ref),
        ]
    ):
        loads[name] = pltpu.make_async_copy(src, dst, load_sem.at[number])
        loads[name].start()

    def products(layer, keep):
        loads["grad%d" % layer].wait()
        cot[...] = lax.dot_general(
            by_row_ref[...], grad_ref[layer], (((1,), (1,)), ((), ())), preferred_element_type=F32
        ).astype(BF16)
        loads["latent%d" % layer].wait()
        for first in range(0, group, 4):
            product = jnp.dot(
                cot[first * rows : (first + 4) * rows], latent_ref[layer], preferred_element_type=F32
            )
            keep(slice(first, first + 4), product.astype(BF16).reshape(4, rows, width))

    def keep_0(blocks_of, product):
        part_a[blocks_of] = product

    def keep_1(blocks_of, product):
        part_b[blocks_of] = product[:, :, :narrow]
        for way in range(2):
            begin = narrow + way * extra
            part_x[way, blocks_of, :, half:] = product[:, :, begin : begin + extra]

    def keep_2(blocks_of, product):
        for way in range(2):
            part_x[way, blocks_of, :, :half] = product[:, :, way * half : (way + 1) * half]

    near, far = ring // 2 - 1, ring // 2

    def hops(way, lane):
        return far if way == lane else near

    def chunk_at(way, distance):
        if way == 0:
            return lax.rem(z + distance, ring)
        return lax.rem(z + ring - distance, ring)

    def ring_copy(kind, way, lane, step):
        chunk = chunk_at(way, hops(way, lane) - step)
        src, dst, send, got = {
            "a": (part_a.at[chunk * X_HI + lane], ring_a, send_a, got_a),
            "b": (part_b.at[chunk * X_HI + lane], ring_b, send_b, got_b),
            "x": (part_x.at[lane, chunk * X_HI + side], ring_x, send_x, got_x),
        }[kind]
        return remote(
            src,
            dst.at[step, way, lane],
            send.at[step, way, lane],
            got.at[step, way, lane],
            up if way == 0 else down,
        )

    cross_order = [(0, far)]
    for distance in range(near, 0, -1):
        cross_order += [(0, distance), (1, distance)]
    cross_order.append((0, 0))

    def cross_copy(place, lane):
        chunk = chunk_at(*cross_order[place])
        return remote(
            part_x.at[lane, chunk * X_HI + 1 - side],
            cross_x.at[lane, chunk],
            send_c.at[place, lane],
            got_c.at[place, lane],
            partner,
        )

    def pair_copy(kind):
        number, src, dst = {"a": (0, part_a, pair_a), "b": (1, part_b, pair_b)}[kind]
        return remote(src.at[partner], dst, send_p.at[number], got_p.at[number], partner)

    def cross(first, last):
        for place in range(first, last):
            for lane in range(2):
                cross_copy(place, lane).start()

    def ring_step(kind, way, lane, step):
        count = hops(way, lane)
        if step >= 0:
            ring_copy(kind, way, lane, step).wait_recv()
        if step == count - 1:
            return
        distance = count - step - 1
        chunk = chunk_at(way, distance)
        if kind == "x":
            place = cross_order.index((0 if distance == far else way, distance))
            cross_copy(place, lane).wait_recv()
            spot = chunk * X_HI + side
            value = part_x[lane, spot].astype(F32) + cross_x[lane, chunk].astype(F32)
            if step >= 0:
                value = value + ring_x[step, way, lane].astype(F32)
            part_x[lane, spot] = value.astype(BF16)
        elif step >= 0:
            mine, came = {"a": (part_a, ring_a), "b": (part_b, ring_b)}[kind]
            spot = chunk * X_HI + lane
            mine[spot] = (mine[spot].astype(F32) + came[step, way, lane].astype(F32)).astype(BF16)
        ring_copy(kind, way, lane, step + 1).start()

    def ring_far(kind, step):
        for way in range(2):
            ring_step(kind, way, way, step)

    def ring_near(kind, step):
        for way in range(2):
            ring_step(kind, way, 1 - way, step)

    def arrived(kind, lane):
        came = {"a": ring_a, "b": ring_b}[kind]
        if isinstance(lane, int):
            up_last, down_last = hops(0, lane) - 1, hops(1, lane) - 1
        else:
            up_last, down_last = far - 1 - lane, near - 1 + lane
        return came[up_last, 0, lane].astype(F32) + came[down_last, 1, lane].astype(F32)

    def pair_step(kind):
        mine = {"a": part_a, "b": part_b}[kind]
        mine[partner] = (mine[partner].astype(F32) + arrived(kind, 1 - side)).astype(BF16)
        pair_copy(kind).start()

    loads["by_row"].wait()
    products(0, keep_0)
    pl.semaphore_wait(barrier, 3)
    ring_far("a", -1)
    ring_near("a", -1)
    products(2, keep_2)
    products(1, keep_1)
    cross(0, 1)
    ring_far("b", -1)
    ring_near("b", -1)
    cross(1, 3)

    owner_of = [owner_ref[m // heads, m % heads] for m in range(mats)]
    slot_of = []
    for m in range(mats):
        slot = jnp.int32(0)
        for earlier in range(m):
            slot = slot + jnp.where(owner_of[earlier] == owner_of[m], 1, 0)
        slot_of.append(slot)

    @pl.loop(0, group)
    def _(owner):
        for slot in range(CAP):
            found = jnp.int32(mats)
            for m in range(mats):
                found = jnp.where((owner_of[m] == owner) & (slot_of[m] == slot), m, found)
            pick[slot, owner] = found

    ring_far("a", 0)
    ring_near("a", 0)
    ring_far("b", 0)
    ring_near("b", 0)
    ring_far("x", -1)
    cross(3, 5)
    ring_far("a", 1)
    ring_near("a", 1)
    ring_far("b", 1)
    ring_near("b", 1)
    ring_far("x", 0)
    ring_near("x", -1)
    cross(5, 7)
    ring_far("a", 2)
    ring_near("a", 2)
    ring_far("b", 2)
    ring_near("b", 2)
    ring_far("x", 1)
    ring_near("x", 0)
    cross(7, 8)
    ring_far("a", 3)
    pair_step("a")
    ring_far("b", 3)
    pair_step("b")
    ring_far("x", 2)
    ring_near("x", 1)
    ring_far("x", 3)
    ring_near("x", 2)
    for lane in range(2):
        cross_copy(ring - 1, lane).wait_recv()

    loads["momentum"].wait()
    loads["split"].wait()

    def last_sum(kind):
        mine, other = {"a": (part_a, pair_a), "b": (part_b, pair_b)}[kind]
        pair_copy(kind).wait_recv()
        return mine[me].astype(F32) + arrived(kind, side) + other[...].astype(F32)

    def last_sum_x(lane, columns):
        return (
            part_x[lane, me, :, columns].astype(F32)
            + cross_x[lane, z, :, columns].astype(F32)
            + ring_x[hops(0, lane) - 1, 0, lane, :, columns].astype(F32)
            + ring_x[hops(1, lane) - 1, 1, lane, :, columns].astype(F32)
        )

    def work_of(device):
        return jnp.minimum(device % 4, 2) * heads + device // 4

    def work_copy(layer, head):
        mat = layer * heads + head
        return remote(
            blocks.at[mat], worked.at[me], send_work.at[mat], got_work.at[me], worker_of(layer, head)
        )

    def work_from(source):
        return remote(worked.at[source], worked.at[source], send_work.at[0], got_work.at[source], up)

    lot = me % 4
    works = (lot < 2) | (lot == 2 + (me // 4) % 2)
    mine = work_of(me)

    for layer in (2, 0, 1):
        if layer == 2:
            for way in range(2):
                total[:, way * half : (way + 1) * half] = last_sum_x(way, slice(0, half))
        elif layer == 0:
            total[...] = last_sum("a")
        else:
            total[:, :narrow] = last_sum("b")
            for way in range(2):
                begin = narrow + way * extra
                total[:, begin : begin + extra] = last_sum_x(way, slice(half, half + extra))
        for row in range(rows_q):
            span = slice(row * heads, (row + 1) * heads)
            fresh = DECAY_RATE * momentum_ref[layer, row] + total[span, :]
            new_momentum_ref[layer, row] = fresh
            total[span, :] = fresh
        stacked = jnp.concatenate(
            [total[:, q * quarter : (q + 1) * quarter].astype(BF16) for q in range(4)], axis=0
        )
        blocks[layer * heads : (layer + 1) * heads] = (
            jnp.dot(split_ref[...], stacked, preferred_element_type=F32)
            .astype(BF16)
            .reshape(heads, rows, quarter)
        )
        for head in range(heads):

            @pl.when(me != worker_of(layer, head))
            def _():
                work_copy(layer, head).start()

    blocks[mats] = jnp.zeros((rows, quarter), BF16)

    stores = [pltpu.make_async_copy(new_momentum_ref, new_momentum_hbm, store_sem.at[0])]
    stores[0].start()

    def back_copy(mat, step):
        peer = lax.rem(me + step, group)
        return remote(back.at[peer], returned.at[mat], send_back.at[step], got_back.at[mat], peer)

    def out_copy(slot, step):
        peer = lax.rem(me + step, group)
        return remote(
            outgoing.at[slot, peer],
            incoming.at[slot, me],
            send_out.at[slot, step],
            got_out.at[slot, step],
            peer,
        )

    def send_slot(slot):
        @pl.loop(1, group)
        def _(step):
            peer = lax.rem(me + step, group)
            outgoing[slot, peer] = blocks[pick[slot, peer]]
            out_copy(slot, step).start()

        incoming[slot, me] = blocks[pick[slot, me]]

    def work_left():
        for layer in range(layers):
            for head in range(heads):

                @pl.when(me != worker_of(layer, head))
                def _():
                    work_copy(layer, head).wait_send()

    def slot_left(slot, first, last):
        @pl.loop(first, last)
        def _(step):
            out_copy(slot, step).wait_send()

    def do_work():
        @pl.when(works)
        def _():
            worked[me] = blocks[mine]

            @pl.loop(1, group)
            def _(step):
                work_from(lax.rem(me + step, group)).wait_recv()

            orthogonalize(worked[...].reshape(group * rows, quarter), gather_ref, shuffled)
            back[...] = (
                jnp.dot(spread_ref[...], shuffled[...], preferred_element_type=F32)
                .astype(BF16)
                .reshape(group, rows, quarter)
            )

    def post_back():
        @pl.when(works)
        def _():
            @pl.loop(1, group)
            def _(step):
                back_copy(mine, step).start()

            returned[mine] = back[me]

    loads["gather"].wait()
    loads["spread"].wait()
    loads["join"].wait()

    def own_slot(slot):
        @pl.loop(1, group)
        def _(step):
            out_copy(slot, step).wait_recv()

        orthogonalize(incoming[slot].reshape(group * rows, quarter), gather_ref, shuffled)
        for q in range(4):
            owned_ref[slot, :, q * quarter : (q + 1) * quarter] = shuffled[
                q * full_rows : (q + 1) * full_rows
            ]
        stores.append(
            pltpu.make_async_copy(owned_ref.at[slot], owned_hbm.at[slot], store_sem.at[1 + slot])
        )
        stores[-1].start()

    send_slot(0)
    work_left()
    send_slot(1)
    do_work()
    own_slot(0)
    slot_left(0, 1, group)
    slot_left(1, 1, group // 2)
    post_back()
    own_slot(1)
    slot_left(1, group // 2, group)

    for layer in range(layers):
        for head in range(heads):
            mat = layer * heads + head

            @pl.when(me != worker_of(layer, head))
            def _():
                back_copy(mat, 1).wait_recv()

        gathered = returned[layer * heads : (layer + 1) * heads].reshape(4 * rows, quarter)
        turned[...] = jnp.dot(join_ref[...], gathered, preferred_element_type=F32)
        for row in range(rows_q):
            for q in range(4):
                begin = q * rows + row * heads
                update_ref[layer, row, :, q * quarter : (q + 1) * quarter] = turned[
                    begin : begin + heads, :
                ]
        stores.append(
            pltpu.make_async_copy(
                update_ref.at[layer], update_hbm.at[layer], store_sem.at[1 + CAP + layer]
            )
        )
        stores[-1].start()

    for kind in "abx":
        for way in range(2):
            for lane in range(2):
                for step in range(hops(way, lane)):
                    ring_copy(kind, way, lane, step).wait_send()
    for place in range(ring):
        for lane in range(2):
            cross_copy(place, lane).wait_send()
    for kind in "ab":
        pair_copy(kind).wait_send()
    @pl.when(works)
    def _():
        @pl.loop(1, group)
        def _(step):
            back_copy(mine, step).wait_send()

    for store in stores:
        store.wait()


def finish(
    update_hbm, new_momentum_hbm, owned_hbm, weight_hbm, logit_ref,
    update_out, weight_out, new_momentum_out, owned_out,
    update, weight, new_weight, new_momentum, owned, load_sem, store_sem,
):
    layers, rows_q, heads, width = weight.shape
    full_rows = owned.shape[1]
    step_scale = LEARN_RATE * RMS_FACTOR * math.sqrt(max(full_rows, width))
    first_row = lax.axis_index("dp") * rows_q
    loads, stores = {}, {}
    for number, (name, src, via, dst) in enumerate(
        [
            ("update", update_hbm, update, update_out),
            ("weight", weight_hbm, weight, None),
            ("new_momentum", new_momentum_hbm, new_momentum, new_momentum_out),
            ("owned", owned_hbm, owned, owned_out),
        ]
    ):
        for part in range(via.shape[0]):
            loads[name, part] = pltpu.make_async_copy(
                src.at[part], via.at[part], load_sem.at[number, part]
            )
            loads[name, part].start()
            if dst is not None:
                stores[name, part] = pltpu.make_async_copy(
                    via.at[part], dst.at[part], store_sem.at[number, part]
                )
    on_diagonal = lax.broadcasted_iota(jnp.int32, (heads, heads), 0) == lax.broadcasted_iota(
        jnp.int32, (heads, heads), 1
    )
    for layer in range(layers):
        clip = jnp.minimum(1.0, CLIP_LIMIT / logit_ref[layer : layer + 1, :])
        clip = jnp.sum(
            jnp.where(on_diagonal, jnp.broadcast_to(clip, (heads, heads)), 0.0),
            axis=1,
            keepdims=True,
        )
        root = jnp.sqrt(clip)
        loads["update", layer].wait()
        stores["update", layer].start()
        loads["weight", layer].wait()
        for row in range(rows_q):
            scale = jnp.where(first_row + row < NOPE, root, clip)
            new_weight[layer, row] = (
                weight[layer, row] * (1.0 - LEARN_RATE * WEIGHT_DECAY)
                - step_scale * update[layer, row]
            ) * scale
        stores["weight", layer] = pltpu.make_async_copy(
            new_weight.at[layer], weight_out.at[layer], store_sem.at[1, layer]
        )
        stores["weight", layer].start()
    for name in ("new_momentum", "owned"):
        for part in range({"new_momentum": layers, "owned": CAP}[name]):
            loads[name, part].wait()
            stores[name, part].start()
    for store in stores.values():
        store.wait()


def on_device(latent, query_grad, momentum, weight, max_logit, owner_list):
    group = lax.axis_size("dp")
    layers, heads, rows_q, width = momentum.shape
    mats = layers * heads
    full_rows = rows_q * group
    rows = heads * rows_q
    quarter = width // 4
    half = width // 2
    ring = group // X_HI
    extra = width // 3
    narrow = width - 2 * extra
    wide = half + extra

    by_row = jnp.asarray(reorder_matrix((heads, group, rows_q), (1, 2, 0)), BF16)
    gather = jnp.asarray(reorder_matrix((group, 4, rows_q), (1, 0, 2)), BF16)
    spread = jnp.asarray(reorder_matrix((4, group, rows_q), (1, 0, 2)), BF16)
    split = jnp.asarray(reorder_matrix((4 * rows_q, heads), (1, 0)), BF16)
    join = jnp.asarray(reorder_matrix((heads, 4 * rows_q), (1, 0)), BF16)

    vmem = pl.BlockSpec(memory_space=pltpu.VMEM)
    smem = pl.BlockSpec(memory_space=pltpu.SMEM)
    hbm = pl.BlockSpec(memory_space=pl.ANY)
    by_rows = (layers, rows_q, heads, width)
    dma = pltpu.SemaphoreType.DMA
    new_momentum, owned, update = pl.pallas_call(
        functools.partial(kernel, group),
        out_shape=(
            jax.ShapeDtypeStruct(by_rows, F32),
            jax.ShapeDtypeStruct((CAP, full_rows, width), BF16),
            jax.ShapeDtypeStruct(by_rows, F32),
        ),
        in_specs=[hbm] * 8 + [smem],
        out_specs=(hbm, hbm, hbm),
        scratch_shapes=[
            pltpu.VMEM(by_rows, F32),
            pltpu.VMEM((CAP, full_rows, width), BF16),
            pltpu.VMEM(by_rows, F32),
            pltpu.VMEM(latent.shape, BF16),
            pltpu.VMEM(query_grad.shape, BF16),
            pltpu.VMEM(by_rows, F32),
            pltpu.VMEM(by_row.shape, BF16),
            pltpu.VMEM(gather.shape, BF16),
            pltpu.VMEM(spread.shape, BF16),
            pltpu.VMEM(split.shape, BF16),
            pltpu.VMEM(join.shape, BF16),
            pltpu.VMEM((heads * full_rows, latent.shape[1]), BF16),
            pltpu.VMEM((group, rows, width), BF16),
            pltpu.VMEM((group, rows, narrow), BF16),
            pltpu.VMEM((2, group, rows, wide), BF16),
            pltpu.VMEM((ring // 2, 2, 2, rows, width), BF16),
            pltpu.VMEM((ring // 2, 2, 2, rows, narrow), BF16),
            pltpu.VMEM((ring // 2, 2, 2, rows, wide), BF16),
            pltpu.VMEM((2, ring, rows, wide), BF16),
            pltpu.VMEM((rows, width), BF16),
            pltpu.VMEM((rows, narrow), BF16),
            pltpu.VMEM((rows, width), F32),
            pltpu.VMEM((4 * rows, quarter), F32),
            pltpu.SMEM((CAP, group), jnp.int32),
            pltpu.VMEM((mats + 1, rows, quarter), BF16),
            pltpu.VMEM((CAP, group, rows, quarter), BF16),
            pltpu.VMEM((CAP, group, rows, quarter), BF16),
            pltpu.VMEM((group * rows, quarter), BF16),
            pltpu.VMEM((group, rows, quarter), BF16),
            pltpu.VMEM((group, rows, quarter), BF16),
            pltpu.VMEM((mats, rows, quarter), BF16),
            dma((12,)),
            dma((ring // 2, 2, 2)),
            dma((ring // 2, 2, 2)),
            dma((ring // 2, 2, 2)),
            dma((ring // 2, 2, 2)),
            dma((ring // 2, 2, 2)),
            dma((ring // 2, 2, 2)),
            dma((ring, 2)),
            dma((ring, 2)),
            dma((2,)),
            dma((2,)),
            dma((CAP, group)),
            dma((CAP, group)),
            dma((mats,)),
            dma((group,)),
            dma((group,)),
            dma((mats,)),
            dma((1 + CAP + layers,)),
        ],
        compiler_params=pltpu.CompilerParams(
            collective_id=0, has_side_effects=True, vmem_limit_bytes=56 * 2**20
        ),
    )(
        latent, query_grad, momentum.transpose(0, 2, 1, 3), by_row, gather, spread, split, join, owner_list
    )

    update, new_weight, new_momentum, owned = pl.pallas_call(
        finish,
        out_shape=(
            jax.ShapeDtypeStruct(by_rows, F32),
            jax.ShapeDtypeStruct(by_rows, F32),
            jax.ShapeDtypeStruct(by_rows, F32),
            jax.ShapeDtypeStruct((CAP, full_rows, width), BF16),
        ),
        in_specs=[hbm] * 4 + [vmem],
        out_specs=(hbm, hbm, hbm, hbm),
        scratch_shapes=[
            pltpu.VMEM(by_rows, F32),
            pltpu.VMEM(by_rows, F32),
            pltpu.VMEM(by_rows, F32),
            pltpu.VMEM(by_rows, F32),
            pltpu.VMEM((CAP, full_rows, width), BF16),
            dma((4, layers)),
            dma((4, layers)),
        ],
        compiler_params=pltpu.CompilerParams(vmem_limit_bytes=56 * 2**20),
    )(update, new_momentum, owned, weight.transpose(0, 2, 1, 3), max_logit)
    return (
        update.transpose(0, 2, 1, 3),
        new_weight.transpose(0, 2, 1, 3),
        new_momentum.transpose(0, 2, 1, 3),
        owned[None],
    )


def solution(mesh):
    placed = (
        P(None, "dp", None),
        P(None, "dp", "expert"),
        P(None, "expert", "dp", None),
        P(None, "expert", "dp", None),
        P(None, "expert"),
        P(None, "expert"),
    )
    return jax.shard_map(
        on_device,
        mesh=mesh,
        in_specs=placed,
        out_specs=(
            P(None, "expert", "dp", None),
            P(None, "expert", "dp", None),
            P(None, "expert", "dp", None),
            P("expert", "dp", None, None),
        ),
        check_vma=False,
    )
```

profile of v0, /device:TPU:8, one launch (start us, length us, event | category | flops | bytes accessed | tf_op | source)
XLA Modules:
  0.0 122.3 jit_solution(12627063105937828913)
XLA Ops:
  0.6 117.5 %shard_map.138 = (f32[3,12,4,1536]{3,2,1,0:T(4,128)}, bf16[2,192,1536]{2,1,0:T(8,128)(2,1)}, f32[3,12,4,1536]{3,2,1,0:T(4,128)}) custom-call(bf16[3,512,1536]{2,1,0:T(8,128)(2,1)} %latent_hbm.1, bf16[3,512,768]{2,1,0:T(8,128)(2,1)} %grad_hbm.1, f32[3,12,4,1536]{3,2,1,0:T(4,128)} %bitcast.6, bf16[768,768]{1,0:T(8,128)(2,1)} %constant.10.clone.by_row_hbm, ...), custom_call_target="tpu_custom_call" | custom-call | tf_op jit(solution)/shard_map/pallas_call | solution.py:611
  118.1 4.0 %shard_map.139 = (f32[3,12,4,1536]{3,2,1,0:T(4,128)}, f32[3,12,4,1536]{3,2,1,0:T(4,128)}, f32[3,12,4,1536]{3,2,1,0:T(4,128)}, bf16[2,192,1536]{2,1,0:T(8,128)(2,1)}) custom-call(f32[3,12,4,1536]{3,2,1,0:T(4,128)} %get-tuple-element.11.update_hbm, f32[3,12,4,1536]{3,2,1,0:T(4,128)} %get-tuple-element.12.new_momentum_hbm, ...), custom_call_target="tpu_custom_call" | custom-call | tf_op jit(solution)/shard_map/pallas_call | solution.py:678
where the time goes:
time: 124 us; the launch traced here: 122 us
  Pallas kernels  121 us (98%)
    pallas_call x1, Pallas kernels, on_device(): pl.pallas_call(functools.partial(kernel, group), out_shape=(jax.ShapeDtyp...  118 us
    pallas_call x1, Pallas kernels, on_device(): pl.pallas_call(finish, out_shape=(jax.ShapeDtypeStruct(by_rows, F32), jax...  3.97 us

commit v1 on v0

--- a/solution.py
+++ b/solution.py
@@ -47,8 +47,25 @@
     )
 
 
-def full_dot(left, right):
-    return jnp.dot(left, right, precision=lax.Precision.HIGHEST, preferred_element_type=F32)
+def parts_of(value, count):
+    parts = []
+    for _ in range(count):
+        parts.append(value.astype(BF16))
+        value = value - parts[-1].astype(F32)
+    return parts
+
+
+def part_dot(left, right):
+    size = left[0].shape[0]
+    count = len(right)
+    result = None
+    for place in range(count - 1, -1, -1):
+        stacked = left[0] if place == count - 1 else jnp.concatenate(left[: count - place], axis=0)
+        product = jnp.dot(stacked, right[place], preferred_element_type=F32)
+        for row in range(count - place - 1, -1, -1):
+            term = product[row * size : (row + 1) * size]
+            result = term if result is None else result + term
+    return result
 
 
 def polynomial(gram):
@@ -58,10 +75,15 @@
     eye = jnp.where(rows == columns, 1.0, 0.0).astype(F32)
     total = None
     for sweep in range(ITERS):
-        mixing = COEF_LINEAR * eye + COEF_CUBIC * gram + COEF_QUINTIC * full_dot(gram, gram)
-        total = mixing if total is None else full_dot(mixing, total)
+        count = 3 if sweep < 3 else 2
+        gram_parts = parts_of(gram, count)
+        mixing = (
+            COEF_LINEAR * eye + COEF_CUBIC * gram + COEF_QUINTIC * part_dot(gram_parts, gram_parts)
+        )
+        mixing_parts = parts_of(mixing, count)
         if sweep < ITERS - 1:
-            gram = full_dot(full_dot(mixing, gram), mixing)
+            gram = part_dot(parts_of(part_dot(mixing_parts, gram_parts), count), mixing_parts)
+        total = mixing if total is None else part_dot(parts_of(total, 2), mixing_parts[:2])
     return total
 
 
@@ -99,14 +121,15 @@
 
 def kernel(
     group,
-    latent_hbm, grad_hbm, momentum_hbm, by_row_hbm, gather_hbm, spread_hbm, split_hbm, join_hbm, owner_ref,
-    new_momentum_hbm, owned_hbm, update_hbm,
-    new_momentum_ref, owned_ref, update_ref,
+    latent_hbm, grad_hbm, momentum_hbm, weight_hbm, by_row_hbm, gather_hbm, spread_hbm, split_hbm, join_hbm,
+    logit_ref, owner_ref,
+    new_momentum_ref, owned_ref, update_ref, new_weight_ref,
+    weight_ref,
     latent_ref, grad_ref, momentum_ref, by_row_ref, gather_ref, spread_ref, split_ref, join_ref,
     cot, part_a, part_b, part_x, ring_a, ring_b, ring_x, cross_x, pair_a, pair_b,
     total, turned, pick, blocks, outgoing, incoming, shuffled, worked, back, returned,
     load_sem, send_a, got_a, send_b, got_b, send_x, got_x, send_c, got_c, send_p, got_p,
-    send_out, got_out, send_work, got_work, send_back, got_back, store_sem,
+    send_out, got_out, send_work, got_work, send_back, got_back,
 ):
     layers, rows_q, heads, width = momentum_ref.shape
     rows = heads * rows_q
@@ -143,6 +166,7 @@
             ("gather", gather_hbm, gather_ref),
             ("spread", spread_hbm, spread_ref),
             ("join", join_hbm, join_ref),
+            ("weight", weight_hbm, weight_ref),
         ]
     ):
         loads[name] = pltpu.make_async_copy(src, dst, load_sem.at[number])
@@ -388,8 +412,6 @@
 
     blocks[mats] = jnp.zeros((rows, quarter), BF16)
 
-    stores = [pltpu.make_async_copy(new_momentum_ref, new_momentum_hbm, store_sem.at[0])]
-    stores[0].start()
 
     def back_copy(mat, step):
         peer = lax.rem(me + step, group)
@@ -466,10 +488,6 @@
             owned_ref[slot, :, q * quarter : (q + 1) * quarter] = shuffled[
                 q * full_rows : (q + 1) * full_rows
             ]
-        stores.append(
-            pltpu.make_async_copy(owned_ref.at[slot], owned_hbm.at[slot], store_sem.at[1 + slot])
-        )
-        stores[-1].start()
 
     send_slot(0)
     work_left()
@@ -477,11 +495,15 @@
     do_work()
     own_slot(0)
     slot_left(0, 1, group)
-    slot_left(1, 1, group // 2)
+    slot_left(1, 1, group)
     post_back()
     own_slot(1)
-    slot_left(1, group // 2, group)
-
+
+    loads["weight"].wait()
+    step_scale = LEARN_RATE * RMS_FACTOR * math.sqrt(max(full_rows, width))
+    heads_diagonal = lax.broadcasted_iota(jnp.int32, (heads, heads), 0) == lax.broadcasted_iota(
+        jnp.int32, (heads, heads), 1
+    )
     for layer in range(layers):
         for head in range(heads):
             mat = layer * heads + head
@@ -492,18 +514,24 @@
 
         gathered = returned[layer * heads : (layer + 1) * heads].reshape(4 * rows, quarter)
         turned[...] = jnp.dot(join_ref[...], gathered, preferred_element_type=F32)
+        clip = jnp.minimum(1.0, CLIP_LIMIT / logit_ref[layer : layer + 1, :])
+        clip = jnp.sum(
+            jnp.where(heads_diagonal, jnp.broadcast_to(clip, (heads, heads)), 0.0),
+            axis=1,
+            keepdims=True,
+        )
+        root = jnp.sqrt(clip)
         for row in range(rows_q):
+            scale = jnp.where(me * rows_q + row < NOPE, root, clip)
             for q in range(4):
                 begin = q * rows + row * heads
-                update_ref[layer, row, :, q * quarter : (q + 1) * quarter] = turned[
-                    begin : begin + heads, :
-                ]
-        stores.append(
-            pltpu.make_async_copy(
-                update_ref.at[layer], update_hbm.at[layer], store_sem.at[1 + CAP + layer]
-            )
-        )
-        stores[-1].start()
+                columns = slice(q * quarter, (q + 1) * quarter)
+                fresh = turned[begin : begin + heads, :]
+                update_ref[layer, row, :, columns] = fresh
+                new_weight_ref[layer, row, :, columns] = (
+                    weight_ref[layer, row, :, columns] * (1.0 - LEARN_RATE * WEIGHT_DECAY)
+                    - step_scale * fresh
+                ) * scale
 
     for kind in "abx":
         for way in range(2):
@@ -521,67 +549,18 @@
         def _(step):
             back_copy(mine, step).wait_send()
 
-    for store in stores:
-        store.wait()
-
-
-def finish(
-    update_hbm, new_momentum_hbm, owned_hbm, weight_hbm, logit_ref,
-    update_out, weight_out, new_momentum_out, owned_out,
-    update, weight, new_weight, new_momentum, owned, load_sem, store_sem,
-):
-    layers, rows_q, heads, width = weight.shape
-    full_rows = owned.shape[1]
-    step_scale = LEARN_RATE * RMS_FACTOR * math.sqrt(max(full_rows, width))
-    first_row = lax.axis_index("dp") * rows_q
-    loads, stores = {}, {}
-    for number, (name, src, via, dst) in enumerate(
-        [
-            ("update", update_hbm, update, update_out),
-            ("weight", weight_hbm, weight, None),
-            ("new_momentum", new_momentum_hbm, new_momentum, new_momentum_out),
-            ("owned", owned_hbm, owned, owned_out),
-        ]
-    ):
-        for part in range(via.shape[0]):
-            loads[name, part] = pltpu.make_async_copy(
-                src.at[part], via.at[part], load_sem.at[number, part]
-            )
-            loads[name, part].start()
-            if dst is not None:
-                stores[name, part] = pltpu.make_async_copy(
-                    via.at[part], dst.at[part], store_sem.at[number, part]
-                )
-    on_diagonal = lax.broadcasted_iota(jnp.int32, (heads, heads), 0) == lax.broadcasted_iota(
-        jnp.int32, (heads, heads), 1
-    )
-    for layer in range(layers):
-        clip = jnp.minimum(1.0, CLIP_LIMIT / logit_ref[layer : layer + 1, :])
-        clip = jnp.sum(
-            jnp.where(on_diagonal, jnp.broadcast_to(clip, (heads, heads)), 0.0),
-            axis=1,
-            keepdims=True,
-        )
-        root = jnp.sqrt(clip)
-        loads["update", layer].wait()
-        stores["update", layer].start()
-        loads["weight", layer].wait()
-        for row in range(rows_q):
-            scale = jnp.where(first_row + row < NOPE, root, clip)
-            new_weight[layer, row] = (
-                weight[layer, row] * (1.0 - LEARN_RATE * WEIGHT_DECAY)
-                - step_scale * update[layer, row]
-            ) * scale
-        stores["weight", layer] = pltpu.make_async_copy(
-            new_weight.at[layer], weight_out.at[layer], store_sem.at[1, layer]
-        )
-        stores["weight", layer].start()
-    for name in ("new_momentum", "owned"):
-        for part in range({"new_momentum": layers, "owned": CAP}[name]):
-            loads[name, part].wait()
-            stores[name, part].start()
-    for store in stores.values():
-        store.wait()
+
+def finish(*refs):
+    kept, outs, sem = refs[:4], refs[4:8], refs[8]
+    copies = [
+        pltpu.make_async_copy(src.at[part], dst.at[part], sem.at[number, part])
+        for number, (src, dst) in enumerate(zip(kept, outs))
+        for part in range(src.shape[0])
+    ]
+    for copy in copies:
+        copy.start()
+    for copy in copies:
+        copy.wait()
 
 
 def on_device(latent, query_grad, momentum, weight, max_logit, owner_list):
@@ -608,18 +587,17 @@
     hbm = pl.BlockSpec(memory_space=pl.ANY)
     by_rows = (layers, rows_q, heads, width)
     dma = pltpu.SemaphoreType.DMA
-    new_momentum, owned, update = pl.pallas_call(
+    new_momentum, owned, update, new_weight = pl.pallas_call(
         functools.partial(kernel, group),
         out_shape=(
-            jax.ShapeDtypeStruct(by_rows, F32),
-            jax.ShapeDtypeStruct((CAP, full_rows, width), BF16),
-            jax.ShapeDtypeStruct(by_rows, F32),
-        ),
-        in_specs=[hbm] * 8 + [smem],
-        out_specs=(hbm, hbm, hbm),
-        scratch_shapes=[
             pltpu.VMEM(by_rows, F32),
             pltpu.VMEM((CAP, full_rows, width), BF16),
+            pltpu.VMEM(by_rows, F32),
+            pltpu.VMEM(by_rows, F32),
+        ),
+        in_specs=[hbm] * 9 + [vmem, smem],
+        out_specs=(vmem, vmem, vmem, vmem),
+        scratch_shapes=[
             pltpu.VMEM(by_rows, F32),
             pltpu.VMEM(latent.shape, BF16),
             pltpu.VMEM(query_grad.shape, BF16),
@@ -649,7 +627,7 @@
             pltpu.VMEM((group, rows, quarter), BF16),
             pltpu.VMEM((group, rows, quarter), BF16),
             pltpu.VMEM((mats, rows, quarter), BF16),
-            dma((12,)),
+            dma((13,)),
             dma((ring // 2, 2, 2)),
             dma((ring // 2, 2, 2)),
             dma((ring // 2, 2, 2)),
@@ -666,13 +644,22 @@
             dma((group,)),
             dma((group,)),
             dma((mats,)),
-            dma((1 + CAP + layers,)),
         ],
         compiler_params=pltpu.CompilerParams(
             collective_id=0, has_side_effects=True, vmem_limit_bytes=56 * 2**20
         ),
     )(
-        latent, query_grad, momentum.transpose(0, 2, 1, 3), by_row, gather, spread, split, join, owner_list
+        latent,
+        query_grad,
+        momentum.transpose(0, 2, 1, 3),
+        weight.transpose(0, 2, 1, 3),
+        by_row,
+        gather,
+        spread,
+        split,
+        join,
+        max_logit,
+        owner_list,
     )
 
     update, new_weight, new_momentum, owned = pl.pallas_call(
@@ -683,19 +670,11 @@
             jax.ShapeDtypeStruct(by_rows, F32),
             jax.ShapeDtypeStruct((CAP, full_rows, width), BF16),
         ),
-        in_specs=[hbm] * 4 + [vmem],
+        in_specs=[hbm] * 4,
         out_specs=(hbm, hbm, hbm, hbm),
-        scratch_shapes=[
-            pltpu.VMEM(by_rows, F32),
-            pltpu.VMEM(by_rows, F32),
-            pltpu.VMEM(by_rows, F32),
-            pltpu.VMEM(by_rows, F32),
-            pltpu.VMEM((CAP, full_rows, width), BF16),
-            dma((4, layers)),
-            dma((4, layers)),
-        ],
-        compiler_params=pltpu.CompilerParams(vmem_limit_bytes=56 * 2**20),
-    )(update, new_momentum, owned, weight.transpose(0, 2, 1, 3), max_logit)
+        scratch_shapes=[dma((4, layers))],
+        compiler_params=pltpu.CompilerParams(vmem_limit_bytes=2 * 2**20),
+    )(update, new_weight, new_momentum, owned)
     return (
         update.transpose(0, 2, 1, 3),
         new_weight.transpose(0, 2, 1, 3),

time: 124 us -> 121 us (0.976)
  Pallas kernels: 121 us -> 118 us
    pallas_call x1, Pallas kernels: 3.97 us -> 1.99 us  [on_device(): pl.pallas_call(finish, out_shape=(jax.ShapeDtypeStruct(by_rows, F32), jax...]
where the time goes in v1:
time: 121 us; the launch traced here: 119 us
  Pallas kernels  118 us (98%)
    pallas_call x1, Pallas kernels, on_device(): pl.pallas_call(functools.partial(kernel, group), out_shape=(pltpu.VMEM(by...  116 us

profile of v1, /device:TPU:8, one launch (start us, length us, event | category | flops | bytes accessed | tf_op | source)
XLA Modules:
  0.0 119.2 jit_solution(8400357825594217548)
XLA Ops:
  0.6 116.4 %shard_map.138 = (f32[3,12,4,1536]{3,2,1,0:T(4,128)S(1)}, bf16[2,192,1536]{2,1,0:T(8,128)(2,1)S(1)}, f32[3,12,4,1536]{3,2,1,0:T(4,128)S(1)}, f32[3,12,4,1536]{3,2,1,0:T(4,128)S(1)}) custom-call(bf16[3,512,1536]{2,1,0:T(8,128)(2,1)} %latent_hbm.1, bf16[3,512,768]{2,1,0:T(8,128)(2,1)} %grad_hbm.1, f32[3,12,4,1536]{3,2,1,0:T(4,128)} %bitcast.6, ...), custom_call_target="tpu_custom_call" | custom-call | tf_op jit(solution)/shard_map/pallas_call | solution.py:590
  117.1 2.0 %shard_map.139 = (f32[3,12,4,1536]{3,2,1,0:T(4,128)}, f32[3,12,4,1536]{3,2,1,0:T(4,128)}, f32[3,12,4,1536]{3,2,1,0:T(4,128)}, bf16[2,192,1536]{2,1,0:T(8,128)(2,1)}) custom-call(f32[3,12,4,1536]{3,2,1,0:T(4,128)S(1)} %get-tuple-element.12.refs_0_, f32[3,12,4,1536]{3,2,1,0:T(4,128)S(1)} %get-tuple-element.13.refs_1_, ...), custom_call_target="tpu_custom_call" | custom-call | tf_op jit(solution)/shard_map/pallas_call | solution.py:665

commit v2 on v1

--- a/solution.py
+++ b/solution.py
@@ -572,7 +572,7 @@
     quarter = width // 4
     half = width // 2
     ring = group // X_HI
-    extra = width // 3
+    extra = width // 4
     narrow = width - 2 * extra
     wide = half + extra
 

time: 121 us -> 120 us (level); the launches traced: 119 us -> 120 us
  no operation moved by 1% of the time
where the time goes in v2:
time: 120 us
  Pallas kernels  119 us (99%)
    pallas_call x1, Pallas kernels, on_device(): pl.pallas_call(functools.partial(kernel, group), out_shape=(pltpu.VMEM(by...  117 us

profile of v2, /device:TPU:8, one launch (start us, length us, event | category | flops | bytes accessed | tf_op | source)
XLA Modules:
  0.0 120.1 jit_solution(2401588523026226055)
XLA Ops:
  0.6 117.3 %shard_map.138 = (f32[3,12,4,1536]{3,2,1,0:T(4,128)S(1)}, bf16[2,192,1536]{2,1,0:T(8,128)(2,1)S(1)}, f32[3,12,4,1536]{3,2,1,0:T(4,128)S(1)}, f32[3,12,4,1536]{3,2,1,0:T(4,128)S(1)}) custom-call(bf16[3,512,1536]{2,1,0:T(8,128)(2,1)} %latent_hbm.1, bf16[3,512,768]{2,1,0:T(8,128)(2,1)} %grad_hbm.1, f32[3,12,4,1536]{3,2,1,0:T(4,128)} %bitcast.6, ...), custom_call_target="tpu_custom_call" | custom-call | tf_op jit(solution)/shard_map/pallas_call | solution.py:590
  118.0 2.0 %shard_map.139 = (f32[3,12,4,1536]{3,2,1,0:T(4,128)}, f32[3,12,4,1536]{3,2,1,0:T(4,128)}, f32[3,12,4,1536]{3,2,1,0:T(4,128)}, bf16[2,192,1536]{2,1,0:T(8,128)(2,1)}) custom-call(f32[3,12,4,1536]{3,2,1,0:T(4,128)S(1)} %get-tuple-element.12.refs_0_, f32[3,12,4,1536]{3,2,1,0:T(4,128)S(1)} %get-tuple-element.13.refs_1_, ...), custom_call_target="tpu_custom_call" | custom-call | tf_op jit(solution)/shard_map/pallas_call | solution.py:665
